TPU v7x, 32 devices: a whole 2x2x4 slice. The times are simulated.
32 devices in a mesh: seq: 8 (over z, y), head: 4 (over x, core).
Axes of the slice: x: 2, y: 2, z: 4, core: 2. Of those that a mesh axis runs over, the one named last changes fastest.
Arguments:
- tokens: bfloat16 [2, 1024, 2560], P(None, 'seq', 'head'), may hold values from -6 to 6
- token_mix: float32 [5, 2560], replicated, may hold values from 0.05 to 0.95
- receptance: bfloat16 [2560, 2560], P(None, 'head'), may hold values from -0.125 to 0.125
- key_weight: bfloat16 [2560, 2560], P(None, 'head'), may hold values from -0.125 to 0.125
- value_weight: bfloat16 [2560, 2560], P(None, 'head'), may hold values from -0.125 to 0.125
- decay_base: float32 [2560], P('head'), may hold values from -12.5 to -1.9
- decay_down_matrix: bfloat16 [2560, 96], replicated, may hold values from -0.125 to 0.125
- decay_up_matrix: bfloat16 [96, 2560], P(None, 'head'), may hold values from -0.625 to 0.625
- learn_base: float32 [2560], P('head'), may hold values from -1.5 to 1.5
- learning_down_matrix: bfloat16 [2560, 96], replicated, may hold values from -0.125 to 0.125
- learning_up_matrix: bfloat16 [96, 2560], P(None, 'head'), may hold values from -0.625 to 0.625
- key_scale: float32 [2560], P('head'), may hold values from 0.25 to 1.75
- key_blend: float32 [2560], P('head'), may hold values from 0.2 to 1
- norm_gain: float32 [2560], P('head'), may hold values from 0.25 to 1.75
- norm_bias: float32 [2560], P('head'), may hold values from -3 to 3
- output_weight: bfloat16 [2560, 2560], P('head'), may hold values from -0.125 to 0.125
Outputs:
- mixed_out: bfloat16 [2, 1024, 2560], P(None, 'seq', 'head')
All inputs are finite; a program needn't handle non-finite values.
Results may differ from a plain program's by a relative error of at most 0.014.
Values may be sent and summed in bfloat16 or wider, within the bound.
A program may use at most 128 MiB of HBM per device.

v0:
```python
import functools
import math

import jax
import jax.numpy as jnp
from jax import lax
from jax.experimental import pallas as pl
from jax.experimental.pallas import tpu as pltpu
from jax.sharding import PartitionSpec as P

HEAD_SIZE = 64
PAIR = 2 * HEAD_SIZE
MESH = pl.DeviceIdType.MESH
F32 = jnp.float32
BF16 = jnp.bfloat16
DECAY_SCALE = math.exp(-0.5)


def dot(left, right):
    return jnp.dot(left, right, preferred_element_type=F32)


def dot_nt(left, right):
    return lax.dot_general(left, right, (((1,), (1,)), ((), ())), preferred_element_type=F32)


def dot_tn(left, right):
    return lax.dot_general(left, right, (((0,), (0,)), ((), ())), preferred_element_type=F32)


def iota(shape, axis):
    return lax.broadcasted_iota(jnp.int32, shape, axis)


def head_sum(values):
    first = iota(values.shape, 1) < HEAD_SIZE
    low = jnp.sum(jnp.where(first, values, 0.0), axis=-1, keepdims=True)
    high = jnp.sum(jnp.where(first, 0.0, values), axis=-1, keepdims=True)
    return jnp.where(first, low, high)


def diagonal(values):
    half = values.shape[1] // 2
    first = iota(values.shape, 1) < half
    zero = jnp.zeros_like(values)
    return jnp.concatenate(
        [jnp.where(first, values, zero), jnp.where(first, zero, values)], axis=0
    )


def chunk_maps(recept, key_raw, value, decay_arg, learn_arg, key_scale, key_blend):
    size = recept.shape[0]
    decay = -DECAY_SCALE / (1.0 + jnp.exp(-decay_arg))
    learn = 1.0 / (1.0 + jnp.exp(-learn_arg))
    scaled = key_raw * key_scale
    unit = scaled * lax.rsqrt(head_sum(scaled * scaled) + 1e-06)
    key = key_raw * (1.0 + (learn - 1.0) * key_blend)
    beta = unit * learn
    lower = (iota((size, size), 0) >= iota((size, size), 1)).astype(BF16)
    coarse = decay.astype(BF16)
    fine = (decay - coarse.astype(F32)).astype(BF16)
    sums = dot(lower, jnp.concatenate([coarse, fine], axis=1))
    cumul = sums[:, :PAIR] + sums[:, PAIR:]
    before = cumul - decay
    middle = cumul[size // 2 - 1 : size // 2, :]
    ending = cumul[size - 1 :, :]
    to_right = jnp.exp(middle - cumul)
    left = jnp.concatenate(
        [-unit * jnp.exp(before - middle), recept * jnp.exp(cumul - middle)], axis=0
    ).astype(BF16)
    with_beta = dot_nt(left, diagonal((beta * to_right).astype(BF16)))
    with_key = dot_nt(left, diagonal((key * to_right).astype(BF16)))
    row = iota((size, 2 * size), 0)
    column = iota((size, 2 * size), 1) % size
    strict = row > column
    within = row >= column
    lower_ab = jnp.where(strict, with_beta[:size], 0.0).astype(BF16)
    lower_ak = jnp.where(strict, with_key[:size], 0.0).astype(BF16)
    lower_rb = jnp.where(within, with_beta[size:], 0.0).astype(BF16)
    lower_rk = jnp.where(within, with_key[size:], 0.0).astype(BF16)
    zero = jnp.zeros_like(lower_ab)
    crossing = row ^ column
    inverse = jnp.where(row == column, 1.0, 0.0) + jnp.where(
        crossing == 1, lower_ab, zero
    ).astype(F32)
    block = 2
    while block < size:
        link = jnp.where((crossing >= block) & (crossing < 2 * block), lower_ab, zero)
        rounded = inverse.astype(BF16)
        half = dot(rounded, diagonal(link)).astype(BF16)
        inverse = inverse + dot(half, diagonal(rounded))
        block *= 2
    value_b = value.astype(BF16)
    from_value = dot(jnp.concatenate([lower_ak, lower_rk], axis=0), diagonal(value_b))
    alpha_exp = (-unit * jnp.exp(before)).astype(BF16)
    gains = dot(
        inverse.astype(BF16),
        jnp.concatenate(
            [diagonal(alpha_exp), diagonal(from_value[:size].astype(BF16))], axis=1
        ),
    )
    gains_b = gains.astype(BF16)
    answers = dot(
        lower_rb,
        jnp.concatenate([diagonal(gains_b[:, :PAIR]), diagonal(gains_b[:, PAIR:])], axis=1),
    )
    query = recept * jnp.exp(cumul) + answers[:, :PAIR]
    local = from_value[size:] + answers[:, PAIR:]
    to_end = jnp.exp(ending - cumul)
    ends = jnp.concatenate([beta * to_end, key * to_end], axis=0)
    sources = jnp.concatenate(
        [gains_b, jnp.concatenate([jnp.zeros_like(value_b), value_b], axis=1)], axis=0
    )
    total = dot(jnp.transpose(ends).astype(BF16), sources)
    same = iota((PAIR, PAIR), 0) == iota((PAIR, PAIR), 1)
    moving = total[:, :PAIR] + jnp.where(same, jnp.exp(ending), 0.0)
    adding = total[:, PAIR:]
    first = iota((HEAD_SIZE, PAIR), 1) < HEAD_SIZE
    map_low = jnp.where(first, moving[:HEAD_SIZE], pltpu.roll(adding[:HEAD_SIZE], HEAD_SIZE, 1))
    map_high = jnp.where(first, pltpu.roll(moving[HEAD_SIZE:], HEAD_SIZE, 1), adding[HEAD_SIZE:])
    return query, local, map_low, map_high


def group_norm(wkv, gain, bias):
    centred = wkv - head_sum(wkv) * (1.0 / HEAD_SIZE)
    spread = head_sum(centred * centred) * (1.0 / HEAD_SIZE)
    return centred * lax.rsqrt(spread + 0.00064) * gain + bias


def mix_kernel(
    seqs,
    axis,
    recept,
    key_raw,
    value,
    decay_hidden,
    learn_hidden,
    decay_up,
    learn_up,
    vectors,
    normed,
    query,
    local,
    maps,
    got,
    states,
    entry,
    map_send,
    map_recv,
    state_send,
    state_recv,
):
    n = lax.axis_size(axis)
    me = lax.axis_index(axis)
    rows, width = recept.shape
    size = rows // seqs
    heads = width // HEAD_SIZE
    slots = maps.shape[0]
    barrier = pltpu.get_barrier_semaphore()
    for d in range(1, n):
        pl.semaphore_signal(
            barrier, inc=1, device_id={axis: lax.rem(me + d, n)}, device_id_type=MESH
        )
    pl.semaphore_wait(barrier, n - 1)
    maps[...] = jnp.zeros_like(maps)

    def one(g, carry):
        lanes = pl.ds(pl.multiple_of(g * PAIR, PAIR), PAIR)
        for s in range(seqs):
            at = pl.ds(s * size, size)
            decay_arg = vectors[0:1, lanes] + dot(decay_hidden[at, :], decay_up[:, lanes])
            learn_arg = vectors[1:2, lanes] + dot(learn_hidden[at, :], learn_up[:, lanes])
            q, out, low, high = chunk_maps(
                recept[at, lanes],
                key_raw[at, lanes],
                value[at, lanes],
                decay_arg,
                learn_arg,
                vectors[2:3, lanes],
                vectors[3:4, lanes],
            )
            query[at, lanes] = q.astype(BF16)
            local[at, lanes] = out
            pair = s * heads + 2 * g
            maps[pair // n, pair % n] = low.astype(BF16)
            maps[(pair + 1) // n, (pair + 1) % n] = high.astype(BF16)
        return carry

    lax.fori_loop(0, width // PAIR, one, 0)

    def exchange(source, target, send, recv):
        copies = []
        for d in range(1, n):
            there = lax.rem(me + d, n)
            copy = pltpu.make_async_remote_copy(
                src_ref=source.at[:, there],
                dst_ref=target.at[:, me],
                send_sem=send.at[d],
                recv_sem=recv.at[d],
                device_id={axis: there},
                device_id_type=MESH,
            )
            copy.start()
            copies.append(copy)
        for slot in range(slots):
            target[slot, me] = source[slot, me]
        for copy in copies:
            copy.wait_recv()
        return copies

    sent_maps = exchange(maps, got, map_send, map_recv)
    pick = (iota((HEAD_SIZE, PAIR), 0) == iota((HEAD_SIZE, PAIR), 1)).astype(BF16)
    first = iota((HEAD_SIZE, PAIR), 1) < HEAD_SIZE
    packed = [jnp.zeros((HEAD_SIZE, PAIR), BF16)] * slots
    for i in range(n):
        for slot in range(slots):
            states[slot, i] = packed[slot]
        if i == n - 1:
            break
        for slot in range(slots):
            after = dot(got[slot, i], jnp.concatenate([packed[slot], pick], axis=0))
            whole = after + pltpu.roll(after, HEAD_SIZE, 1)
            coarse = whole.astype(BF16)
            fine = (whole - coarse.astype(F32)).astype(BF16)
            packed[slot] = jnp.where(first, coarse, fine)
    sent_states = exchange(states, entry, state_send, state_recv)

    def finish(g, carry):
        lanes = pl.ds(pl.multiple_of(g * PAIR, PAIR), PAIR)
        for s in range(seqs):
            at = pl.ds(s * size, size)
            pair = s * heads + 2 * g
            low = entry[pair // n, pair % n]
            high = entry[(pair + 1) // n, (pair + 1) % n]
            zero = jnp.zeros_like(low)
            both = jnp.concatenate(
                [
                    jnp.where(first, low, zero),
                    jnp.where(first, zero, jnp.concatenate([zero[:, :HEAD_SIZE], high[:, :HEAD_SIZE]], axis=1)),
                ],
                axis=0,
            )
            wkv = local[at, lanes] + dot(query[at, lanes], both)
            normed[at, lanes] = group_norm(
                wkv, vectors[4:5, lanes], vectors[5:6, lanes]
            ).astype(BF16)
        return carry

    lax.fori_loop(0, width // PAIR, finish, 0)
    for copy in sent_maps + sent_states:
        copy.wait_send()


def out_kernel(
    axis, normed, weight, out, part, mate_got, across, across_got, mate_send, mate_recv, send, recv
):
    n = lax.axis_size(axis)
    me = lax.axis_index(axis)
    chips = n // 2
    chip, core = me // 2, me % 2
    mate = chip * 2 + (1 - core)
    width = out.shape[1]
    barrier = pltpu.get_barrier_semaphore()
    peers = [mate] + [lax.rem(chip + d, chips) * 2 + core for d in range(1, chips)]
    for peer in peers:
        pl.semaphore_signal(barrier, inc=1, device_id={axis: peer}, device_id_type=MESH)
    pl.semaphore_wait(barrier, chips)

    def columns(index):
        if len(weight.shape) == 3:
            return weight[index]
        return weight[:, pl.ds(pl.multiple_of(index * width, width), width)]

    to_mate = []
    order = list(range(1, chips)) + [0]
    for d in order:
        other = lax.rem(chip + d, chips)
        part[d] = dot(normed[...], columns(other * 2 + 1 - core)).astype(BF16)
        copy = pltpu.make_async_remote_copy(
            src_ref=part.at[d],
            dst_ref=mate_got.at[d],
            send_sem=mate_send.at[d],
            recv_sem=mate_recv.at[d],
            device_id={axis: mate},
            device_id_type=MESH,
        )
        copy.start()
        to_mate.append(copy)
    moving = []
    for step, d in enumerate(order):
        other = lax.rem(chip + d, chips)
        mine = dot(normed[...], columns(other * 2 + core))
        to_mate[step].wait_recv()
        mine = mine + mate_got[d].astype(F32)
        if d == 0:
            break
        across[d] = mine.astype(BF16)
        copy = pltpu.make_async_remote_copy(
            src_ref=across.at[d],
            dst_ref=across_got.at[d],
            send_sem=send.at[d],
            recv_sem=recv.at[d],
            device_id={axis: other * 2 + core},
            device_id_type=MESH,
        )
        copy.start()
        moving.append(copy)
    for step, copy in enumerate(moving):
        copy.wait_recv()
        mine = mine + across_got[step + 1].astype(F32)
    out[...] = mine.astype(BF16)
    for copy in to_mate + moving:
        copy.wait_send()


def vmem():
    return pl.BlockSpec(memory_space=pltpu.VMEM)


def mix(operands, seqs, axis):
    rows, width = operands[0].shape
    n = lax.axis_size(axis)
    pairs = seqs * width // HEAD_SIZE
    slots = -(-pairs // n)
    table = pltpu.VMEM((slots, n, HEAD_SIZE, PAIR), BF16)
    sems = pltpu.SemaphoreType.DMA((n,))
    return pl.pallas_call(
        functools.partial(mix_kernel, seqs, axis),
        out_shape=jax.ShapeDtypeStruct((rows, width), BF16),
        in_specs=[vmem()] * len(operands),
        out_specs=vmem(),
        scratch_shapes=[
            pltpu.VMEM((rows, width), BF16),
            pltpu.VMEM((rows, width), F32),
            table,
            table,
            table,
            table,
            sems,
            sems,
            sems,
            sems,
        ],
        compiler_params=pltpu.CompilerParams(
            collective_id=0, has_side_effects=True, vmem_limit_bytes=48 * 2**20
        ),
    )(*operands)


def project_out(normed, weight, out_width, axis):
    rows = normed.shape[0]
    chips = lax.axis_size(axis) // 2
    table = pltpu.VMEM((chips, rows, out_width), BF16)
    sems = pltpu.SemaphoreType.DMA((chips,))
    return pl.pallas_call(
        functools.partial(out_kernel, axis),
        out_shape=jax.ShapeDtypeStruct((rows, out_width), BF16),
        in_specs=[vmem()] * 2,
        out_specs=vmem(),
        scratch_shapes=[table, table, table, table, sems, sems, sems, sems],
        compiler_params=pltpu.CompilerParams(
            collective_id=1, has_side_effects=True, vmem_limit_bytes=48 * 2**20
        ),
    )(normed, weight)


def body(
    tokens,
    token_mix,
    receptance,
    key_weight,
    value_weight,
    decay_base,
    decay_down_matrix,
    decay_up_matrix,
    learn_base,
    learning_down_matrix,
    learning_up_matrix,
    key_scale,
    key_blend,
    norm_gain,
    norm_bias,
    output_weight,
):
    seqs, length, own_width = tokens.shape
    rows = seqs * length
    lack = -own_width % PAIR
    if lack:
        wider = lambda array: jnp.pad(array, [(0, 0)] * (array.ndim - 1) + [(0, lack)])
        receptance, key_weight, value_weight, decay_up_matrix, learning_up_matrix = map(
            wider, (receptance, key_weight, value_weight, decay_up_matrix, learning_up_matrix)
        )
        decay_base, learn_base, key_scale, key_blend, norm_gain, norm_bias = map(
            wider, (decay_base, learn_base, key_scale, key_blend, norm_gain, norm_bias)
        )
        output_weight = jnp.pad(output_weight, [(0, lack), (0, 0)])
        output_weight = output_weight.reshape(own_width + lack, -1, own_width).transpose(1, 0, 2)
    seq_devices = lax.axis_size("seq")
    boundary = lax.ppermute(
        tokens[:, length - 1 :, :], "seq", [(i, i + 1) for i in range(seq_devices - 1)]
    )
    wide = lax.all_gather(
        jnp.concatenate([boundary, tokens], axis=1), "head", axis=2, tiled=True
    )
    current = wide[:, 1:].astype(F32)
    change = wide[:, :-1].astype(F32) - current
    extent = wide.shape[2]

    def project(which, weight):
        blended = (current + change * token_mix[which]).astype(BF16).reshape(rows, extent)
        return dot(blended, weight)

    decay_hidden = jnp.tanh(project(1, decay_down_matrix)).astype(BF16)
    learn_hidden = project(4, learning_down_matrix).astype(BF16)
    vectors = jnp.stack([decay_base, learn_base, key_scale, key_blend, norm_gain, norm_bias])
    operands = (
        project(0, receptance),
        project(2, key_weight),
        project(3, value_weight),
        decay_hidden,
        learn_hidden,
        decay_up_matrix,
        learning_up_matrix,
        vectors,
    )
    normed = mix(operands, seqs, "seq")
    result = project_out(normed, output_weight, own_width, "head")
    return result.reshape(seqs, length, own_width)


def solution(mesh):
    placed = (
        P(None, "seq", "head"),
        P(),
        P(None, "head"),
        P(None, "head"),
        P(None, "head"),
        P("head"),
        P(),
        P(None, "head"),
        P("head"),
        P(),
        P(None, "head"),
        P("head"),
        P("head"),
        P("head"),
        P("head"),
        P("head", None),
    )
    return jax.shard_map(
        body, mesh=mesh, in_specs=placed, out_specs=P(None, "seq", "head"), check_vma=False
    )
```

profile of v0, /device:TPU:0, one launch (start us, length us, event | category | flops | bytes accessed | tf_op | source)
XLA Modules:
  0.0 117.6 jit_solution(16237542444970455208)
XLA Ops:
  6.5 0.0 copy-start
  6.5 0.0 all-gather.2.cloned.1.call-start
  6.5 0.9 slice.24
  7.4 5.0 %collective-permute-start = (bf16[2,1,640]{2,1,0:T(2,128)(2,1)S(1)}, bf16[2,1,640]{2,1,0:T(2,128)(2,1)S(1)}, u32[]{:S(2)}, u32[]{:S(2)}) collective-permute-start(bf16[2,1,640]{2,1,0:T(2,128)(2,1)S(1)} %slice.24), channel_id=1, source_target_pairs={{0,4},{4,8},{8,12},{12,16},{16,20},{20,24},{24,28},{1,5},{5,9},{9,... | collective-permute-start | bytes 7688 | tf_op jit(solution)/shard_map/ppermute | solution.py:399
  12.4 1.3 %collective-permute-done = bf16[2,1,640]{2,1,0:T(2,128)(2,1)S(1)} collective-permute-done((bf16[2,1,640]{2,1,0:T(2,128)(2,1)S(1)}, bf16[2,1,640]{2,1,0:T(2,128)(2,1)S(1)}, u32[]{:S(2)}, u32[]{:S(2)}) %collective-permute-start) | collective-permute-done | bytes 2592 | tf_op jit(solution)/shard_map/ppermute | solution.py:399
  13.7 1.8 %pad_maximum_fusion = bf16[2,129,640]{2,1,0:T(8,128)(2,1)} fusion(bf16[2,128,640]{2,1,0:T(8,128)(2,1)} %param.16, bf16[2,1,640]{2,1,0:T(2,128)(2,1)S(1)} %collective-permute-done), kind=kLoop, calls=%fused_computation.13 | loop fusion | flops 660480 | bytes 660480 | tf_op jit(solution)/shard_map/concatenate | solution.py:403
  15.5 0.0 all-gather.2.cloned.1.call-update
  15.6 0.7 stack.21
  16.3 0.7 stack.22
  17.0 0.7 stack.23
  17.6 0.7 stack.24
  18.3 0.7 stack.25
  19.0 0.7 stack.26
  19.7 1.3 %slice_reduce_fusion = (f32[2560]{0:T(1024)S(1)}, f32[2560]{0:T(1024)S(1)}, f32[2560]{0:T(1024)S(1)}, f32[2560]{0:T(1024)S(1)}, f32[2560]{0:T(1024)S(1)}) fusion(f32[5,2560]{1,0:T(8,128)} %param.17), kind=kLoop, calls=%fused_computation.14 | loop fusion | bytes 102400 | tf_op jit(solution)/shard_map/slice | solution.py:410
  21.0 15.4 %all-gather.2.cloned.1.call-done = bf16[2,129,2560]{2,1,0:T(8,128)(2,1)} async-done(((bf16[2,129,640]{2,1,0:T(8,128)(2,1)}), bf16[2,129,2560]{2,1,0:T(8,128)(2,1)}) %all-gather.2.cloned.1.call-update) | async-done | bytes 1320976 | tf_op jit(solution)/shard_map/all_gather | solution.py:402
  36.4 0.0 copy-start.6
  36.4 5.6 %fusion.4 = (bf16[2,128,2560]{2,1,0:T(8,128)(2,1)}, bf16[2,128,2560]{2,1,0:T(8,128)(2,1)S(1)}, bf16[2,128,2560]{2,1,0:T(8,128)(2,1)}, bf16[2,128,2560]{2,1,0:T(8,128)(2,1)}, bf16[2,128,2560]{2,1,0:T(8,128)(2,1)}) fusion(f32[2560]{0:T(1024)S(1)} %get-tuple-element.5, bf16[2,129,2560]{2,1,0:T(8,128)(2,1)} %all-gather.2.cloned.1.call-done, ...), kind=kLoop, calls=%fused_computation.10 | loop fusion | flops 11796480 | bytes 9226240 | tf_op jit(solution)/shard_map/convert_element_type | solution.py:410
  42.0 0.0 copy-done.6
  42.0 0.5 convolution_tanh_fusion
  42.6 0.1 copy.19.decay_hidden
  42.7 2.0 %convolution_convert_fusion = bf16[256,96]{0,1:T(8,128)(2,1)S(1)} fusion(bf16[256,2560]{1,0:T(8,128)(2,1)} %bitcast.17, bf16[2560,96]{0,1:T(8,128)(2,1)} %param.25), kind=kOutput, calls=%fused_computation.12 | convolution fusion | flops 125853696 | bytes 1851392 | tf_op jit(solution)/shard_map/dot_general | solution.py:20
  44.6 0.1 copy.20.learn_hidden
  44.8 0.0 copy-done
  44.8 0.0 copy-start.5
  44.8 0.0 copy-start.7
  44.8 2.6 %fusion.5.recept = f32[256,640]{1,0:T(8,128)S(1)} fusion(bf16[256,2560]{1,0:T(8,128)(2,1)} %bitcast.21, bf16[2560,640]{1,0:T(8,128)(2,1)S(1)} %copy-done), kind=kOutput, calls=%fused_computation.19 | convolution fusion | flops 838860800 | bytes 5242880 | tf_op jit(solution)/shard_map/dot_general | solution.py:20
  47.4 0.0 copy-done.5
  47.5 0.0 copy-done.7
  47.5 0.0 copy-start.4
  47.5 0.0 copy-start.8
  47.5 1.2 %fusion.6.key_raw = f32[256,640]{1,0:T(8,128)S(1)} fusion(bf16[256,2560]{1,0:T(8,128)(2,1)S(1)} %bitcast.20, bf16[2560,640]{1,0:T(8,128)(2,1)S(1)} %copy-done.7), kind=kOutput, calls=%fused_computation.20 | convolution fusion | flops 838860800 | bytes 5242880 | tf_op jit(solution)/shard_map/dot_general | solution.py:20
  48.7 0.1 copy-done.4
  48.8 1.0 copy-done.8
  49.8 0.0 copy-start.2
  49.8 0.0 copy-start.3
  49.8 0.0 copy-start.1
  49.8 1.2 %fusion.7.value = f32[256,640]{1,0:T(8,128)S(1)} fusion(bf16[256,2560]{1,0:T(8,128)(2,1)S(1)} %bitcast.19, bf16[2560,640]{1,0:T(8,128)(2,1)S(1)} %copy-done.8), kind=kOutput, calls=%fused_computation.21 | convolution fusion | flops 838860800 | bytes 5242880 | tf_op jit(solution)/shard_map/dot_general | solution.py:20
  51.0 0.0 copy-done.2
  51.0 0.0 copy-done.3
  51.0 47.0 %shard_map.154.normed = bf16[256,640]{1,0:T(8,128)(2,1)S(1)} custom-call(f32[256,640]{1,0:T(8,128)S(1)} %fusion.5.recept, f32[256,640]{1,0:T(8,128)S(1)} %fusion.6.key_raw, f32[256,640]{1,0:T(8,128)S(1)} %fusion.7.value, bf16[256,96]{1,0:T(8,128)(2,1)S(1)} %copy.19.decay_hidden, bf16[256,96]{1,0:T(8,128)(2,1)S(1)} %copy.20.learn_hidden, ...), custom_call_target="tpu_custom_call" | custom-call | tf_op jit(solution)/shard_map/pallas_call | solution.py:327
  98.0 0.0 copy-done.1
  98.1 12.0 %shard_map.155 = bf16[256,640]{1,0:T(8,128)(2,1)S(1)} custom-call(bf16[256,640]{1,0:T(8,128)(2,1)S(1)} %shard_map.154.normed, bf16[640,2560]{1,0:T(8,128)(2,1)S(1)} %copy-done.1), custom_call_target="tpu_custom_call" | custom-call | tf_op jit(solution)/shard_map/pallas_call | solution.py:355
  110.0 0.7 copy.22
  (1 shorter events, 0.0 us)
Async XLA Ops:
  6.5 38.2 %copy-start = (bf16[2560,640]{1,0:T(8,128)(2,1)S(1)}, bf16[2560,640]{1,0:T(8,128)(2,1)}, u32[]{:S(2)}) copy-start(bf16[2560,640]{1,0:T(8,128)(2,1)} %param.18) | copy-start | bytes 9830404
  6.5 29.8 %all-gather.2.cloned.1.call-start = ((), (), s32[]{:S(2)}) async-start(), calls=%async_computation | async-start | bytes 1740800 | tf_op jit(solution)/shard_map/all_gather | solution.py:402
  7.4 6.3 %collective-permute-start = (bf16[2,1,640]{2,1,0:T(2,128)(2,1)S(1)}, bf16[2,1,640]{2,1,0:T(2,128)(2,1)S(1)}, u32[]{:S(2)}, u32[]{:S(2)}) collective-permute-start(bf16[2,1,640]{2,1,0:T(2,128)(2,1)S(1)} %slice.24), channel_id=1, source_target_pairs={{0,4},{4,8},{8,12},{12,16},{16,20},{20,24},{24,28},{1,5},{5,9},{9,... | collective-permute-start | bytes 7688 | tf_op jit(solution)/shard_map/ppermute | solution.py:399
  36.4 5.6 %copy-start.6 = (bf16[2560,96]{0,1:T(8,128)(2,1)S(1)}, bf16[2560,96]{0,1:T(8,128)(2,1)}, u32[]{:S(2)}) copy-start(bf16[2560,96]{0,1:T(8,128)(2,1)} %param.22) | copy-start | bytes 1474564
  44.8 2.7 %copy-start.5 = (bf16[2,128,2560]{2,1,0:T(8,128)(2,1)S(1)}, bf16[2,128,2560]{2,1,0:T(8,128)(2,1)}, u32[]{:S(2)}) copy-start(bf16[2,128,2560]{2,1,0:T(8,128)(2,1)} %get-tuple-element.13) | copy-start | bytes 3932164
  44.8 2.7 %copy-start.7 = (bf16[2560,640]{1,0:T(8,128)(2,1)S(1)}, bf16[2560,640]{1,0:T(8,128)(2,1)}, u32[]{:S(2)}) copy-start(bf16[2560,640]{1,0:T(8,128)(2,1)} %param.19) | copy-start | bytes 9830404
  47.5 1.3 %copy-start.4 = (bf16[2,128,2560]{2,1,0:T(8,128)(2,1)S(1)}, bf16[2,128,2560]{2,1,0:T(8,128)(2,1)}, u32[]{:S(2)}) copy-start(bf16[2,128,2560]{2,1,0:T(8,128)(2,1)} %get-tuple-element.12) | copy-start | bytes 3932164
  47.5 2.3 %copy-start.8 = (bf16[2560,640]{1,0:T(8,128)(2,1)S(1)}, bf16[2560,640]{1,0:T(8,128)(2,1)}, u32[]{:S(2)}) copy-start(bf16[2560,640]{1,0:T(8,128)(2,1)} %param.20) | copy-start | bytes 9830404
  49.8 1.2 %copy-start.2 = (bf16[96,640]{1,0:T(8,128)(2,1)S(1)}, bf16[96,640]{1,0:T(8,128)(2,1)}, u32[]{:S(2)}) copy-start(bf16[96,640]{1,0:T(8,128)(2,1)} %decay_up.1) | copy-start | bytes 368644
  49.8 1.2 %copy-start.3 = (bf16[96,640]{1,0:T(8,128)(2,1)S(1)}, bf16[96,640]{1,0:T(8,128)(2,1)}, u32[]{:S(2)}) copy-start(bf16[96,640]{1,0:T(8,128)(2,1)} %learn_up.1) | copy-start | bytes 368644
  49.8 48.2 %copy-start.1 = (bf16[640,2560]{1,0:T(8,128)(2,1)S(1)}, bf16[640,2560]{1,0:T(8,128)(2,1)}, u32[]{:S(2)}) copy-start(bf16[640,2560]{1,0:T(8,128)(2,1)} %weight.1) | copy-start | bytes 9830404
Sparse Core Ops, SparseCore 0:
  15.7 20.6 all-gather.1
where the time goes:
time: 120 us; the launch traced here: 118 us
  Pallas kernels  59 us (49%)
  waiting for transfers between devices  16.7 us (14%)
  between operations  13.5 us (11%)
  local copies, waits for them, and re-layouts  8.47 us (7%)
  matrix products  7.5 us (6%)
  other arithmetic  7.43 us (6%)
  starting transfers between devices  4.99 us (4%)
    pallas_call x1, Pallas kernels, mix(): pl.pallas_call(functools.partial(mix_kernel, seqs, axis), out_shape=jax.S...  47 us
    all_gather x1, waiting for transfers between devices, body(): lax.all_gather(jnp.concatenate([boundary, tokens], axis=1), 'head', axis=...  15.4 us
    pallas_call x1, Pallas kernels, project_out(): pl.pallas_call(functools.partial(out_kernel, axis), out_shape=jax.ShapeDt...  12 us
    dot_general x5, matrix products, dot(): return jnp.dot(left, right, preferred_element_type=F32)  7.5 us
    convert_element_type x1, other arithmetic, project(): (current + change * token_mix[which]).astype(BF16).reshape(rows, extent)  5.63 us
    ppermute x1, starting transfers between devices, body(): lax.ppermute(tokens[:, length - 1:, :], 'seq', [(i, i + 1) for i in range...  4.99 us
    another operation x7, local copies, waits for them, and re-layouts, body(): jnp.stack([decay_base, learn_base, key_scale, key_blend, norm_gain, norm_...  4.17 us
  transfers between devices with their start and end apart: 2, of which 2 were waited for; matrix products, arithmetic and copies ran while one was open for 5% of the time, Pallas kernels for 0%

commit v1 on v0

v1 whole, which is shorter than its diff:
```python
import math

import jax
import jax.numpy as jnp
from jax import lax
from jax.experimental import pallas as pl
from jax.experimental.pallas import tpu as pltpu
from jax.sharding import PartitionSpec as P

HEAD_SIZE = 64
PAIR = 2 * HEAD_SIZE
MESH = pl.DeviceIdType.MESH
F32 = jnp.float32
BF16 = jnp.bfloat16
DECAY_SCALE = math.exp(-0.5)


def dot(left, right):
    return jnp.dot(left, right, preferred_element_type=F32)


def dot_nt(left, right):
    return lax.dot_general(left, right, (((1,), (1,)), ((), ())), preferred_element_type=F32)


def dot_tn(left, right):
    return lax.dot_general(left, right, (((0,), (0,)), ((), ())), preferred_element_type=F32)


def iota(shape, axis):
    return lax.broadcasted_iota(jnp.int32, shape, axis)


def head_sum(values):
    first = iota(values.shape, 1) < HEAD_SIZE
    low = jnp.sum(jnp.where(first, values, 0.0), axis=-1, keepdims=True)
    high = jnp.sum(jnp.where(first, 0.0, values), axis=-1, keepdims=True)
    return jnp.where(first, low, high)


def diagonal(values):
    half = values.shape[1] // 2
    first = iota(values.shape, 1) < half
    zero = jnp.zeros_like(values)
    return jnp.concatenate(
        [jnp.where(first, values, zero), jnp.where(first, zero, values)], axis=0
    )


def interleaved(units):
    while True:
        results = [next(unit) for unit in units]
        if results[0] is not None:
            return results


def chunk_maps(recept, key_raw, value, decay_arg, learn_arg, key_scale, key_blend):
    size = recept.shape[0]
    decay = -DECAY_SCALE / (1.0 + jnp.exp(-decay_arg))
    learn = 1.0 / (1.0 + jnp.exp(-learn_arg))
    scaled = key_raw * key_scale
    unit = scaled * lax.rsqrt(head_sum(scaled * scaled) + 1e-06)
    key = key_raw * (1.0 + (learn - 1.0) * key_blend)
    beta = unit * learn
    lower = (iota((size, size), 0) >= iota((size, size), 1)).astype(BF16)
    coarse = decay.astype(BF16)
    fine = (decay - coarse.astype(F32)).astype(BF16)
    sums = dot(lower, jnp.concatenate([coarse, fine], axis=1))
    yield
    cumul = sums[:, :PAIR] + sums[:, PAIR:]
    before = cumul - decay
    middle = cumul[size // 2 - 1 : size // 2, :]
    ending = cumul[size - 1 :, :]
    to_right = jnp.exp(middle - cumul)
    left = jnp.concatenate(
        [-unit * jnp.exp(before - middle), recept * jnp.exp(cumul - middle)], axis=0
    ).astype(BF16)
    with_beta = dot_nt(left, diagonal((beta * to_right).astype(BF16)))
    with_key = dot_nt(left, diagonal((key * to_right).astype(BF16)))
    yield
    row = iota((size, 2 * size), 0)
    column = iota((size, 2 * size), 1) % size
    strict = row > column
    within = row >= column
    lower_ab = jnp.where(strict, with_beta[:size], 0.0).astype(BF16)
    lower_ak = jnp.where(strict, with_key[:size], 0.0).astype(BF16)
    lower_rb = jnp.where(within, with_beta[size:], 0.0).astype(BF16)
    lower_rk = jnp.where(within, with_key[size:], 0.0).astype(BF16)
    zero = jnp.zeros_like(lower_ab)
    crossing = row ^ column
    inverse = jnp.where(row == column, 1.0, 0.0) + jnp.where(
        crossing == 1, lower_ab, zero
    ).astype(F32)
    block = 2
    while block < size:
        link = jnp.where((crossing >= block) & (crossing < 2 * block), lower_ab, zero)
        rounded = inverse.astype(BF16)
        half = dot(rounded, diagonal(link)).astype(BF16)
        yield
        inverse = inverse + dot(half, diagonal(rounded))
        yield
        block *= 2
    yield
    value_b = value.astype(BF16)
    from_value = dot(jnp.concatenate([lower_ak, lower_rk], axis=0), diagonal(value_b))
    yield
    alpha_exp = (-unit * jnp.exp(before)).astype(BF16)
    gains = dot(
        inverse.astype(BF16),
        jnp.concatenate(
            [diagonal(alpha_exp), diagonal(from_value[:size].astype(BF16))], axis=1
        ),
    )
    yield
    gains_b = gains.astype(BF16)
    answers = dot(
        lower_rb,
        jnp.concatenate([diagonal(gains_b[:, :PAIR]), diagonal(gains_b[:, PAIR:])], axis=1),
    )
    yield
    query = recept * jnp.exp(cumul) + answers[:, :PAIR]
    local = from_value[size:] + answers[:, PAIR:]
    to_end = jnp.exp(ending - cumul)
    ends = jnp.concatenate([beta * to_end, key * to_end], axis=0)
    sources = jnp.concatenate(
        [gains_b, jnp.concatenate([jnp.zeros_like(value_b), value_b], axis=1)], axis=0
    )
    total = dot(jnp.transpose(ends).astype(BF16), sources)
    yield
    same = iota((PAIR, PAIR), 0) == iota((PAIR, PAIR), 1)
    moving = total[:, :PAIR] + jnp.where(same, jnp.exp(ending), 0.0)
    adding = total[:, PAIR:]
    first = iota((HEAD_SIZE, PAIR), 1) < HEAD_SIZE
    map_low = jnp.where(first, moving[:HEAD_SIZE], pltpu.roll(adding[:HEAD_SIZE], HEAD_SIZE, 1))
    map_high = jnp.where(first, pltpu.roll(moving[HEAD_SIZE:], HEAD_SIZE, 1), adding[HEAD_SIZE:])
    yield query, local, map_low, map_high


def group_norm(wkv, gain, bias):
    centred = wkv - head_sum(wkv) * (1.0 / HEAD_SIZE)
    spread = head_sum(centred * centred) * (1.0 / HEAD_SIZE)
    return centred * lax.rsqrt(spread + 0.00064) * gain + bias


class Remote:
    def __init__(self):
        self.started = []

    def send(self, source, target, send, recv, device):
        copy = pltpu.make_async_remote_copy(
            src_ref=source,
            dst_ref=target,
            send_sem=send,
            recv_sem=recv,
            device_id=device,
            device_id_type=MESH,
        )
        copy.start()
        self.started.append(copy)
        return copy

    def drain(self):
        for copy in self.started:
            copy.wait_send()


def layer_kernel(
    tokens_hbm,
    token_mix,
    weights_hbm,
    downs_hbm,
    ups,
    vectors,
    output_hbm,
    out,
    wide,
    edge,
    weights,
    downs,
    output_weight,
    sums,
    low_sums,
    query,
    local,
    normed,
    maps,
    got,
    states,
    entry,
    part,
    mate_got,
    across,
    across_got,
    load_sem,
    own_sem,
    gather_send,
    gather_recv,
    pass_send,
    pass_recv,
    edge_send,
    edge_recv,
    map_send,
    map_recv,
    state_send,
    state_recv,
    mate_send,
    mate_recv,
    across_send,
    across_recv,
):
    n = lax.axis_size("seq")
    me = lax.axis_index("seq")
    peers = lax.axis_size("head")
    place = lax.axis_index("head")
    chips = peers // 2
    chip, core = place // 2, place % 2
    mate = chip * 2 + 1 - core
    _, seqs, size, own = wide.shape
    width = local.shape[1]
    heads = width // HEAD_SIZE
    slots = maps.shape[0]
    edge_rows = edge.shape[2]
    remote = Remote()

    def at(seq, head):
        return {"seq": seq, "head": head}

    loads = []
    sources = list(weights_hbm) + list(downs_hbm) + [output_hbm]
    targets = list(weights) + list(downs) + [output_weight]
    own_copy = pltpu.make_async_copy(tokens_hbm, wide.at[place], own_sem.at[0])
    own_copy.start()
    for i, (source, target) in enumerate(zip(sources, targets)):
        copy = pltpu.make_async_copy(source, target, load_sem.at[i])
        copy.start()
        loads.append(copy)

    barrier = pltpu.get_barrier_semaphore()

    def greet(seq, head):
        pl.semaphore_signal(barrier, inc=1, device_id=at(seq, head), device_id_type=MESH)

    before, after = lax.rem(me + n - 1, n), lax.rem(me + 1, n)
    for d in range(1, n):
        greet(lax.rem(me + d, n), place)
    greet(me, mate)
    for d in range(1, chips):
        greet(me, lax.rem(chip + d, chips) * 2 + core)
    for d in range(1, peers):
        greet(before, lax.rem(place + d, peers))
    pl.semaphore_wait(barrier, n - 1 + chips + peers - 1)

    from_across = []
    for s in range(seqs):
        for d in range(1, chips):
            copy = remote.send(
                tokens_hbm.at[s],
                wide.at[place, s],
                gather_send.at[d, s],
                gather_recv.at[d, s],
                at(me, lax.rem(chip + d, chips) * 2 + core),
            )
            from_across.append((s, d, copy))
    from_mate = []
    for s in range(seqs):
        from_mate.append(
            remote.send(
                tokens_hbm.at[s],
                wide.at[place, s],
                gather_send.at[0, s],
                gather_recv.at[0, s],
                at(me, mate),
            )
        )
    edges = []
    for d in range(peers):
        edges.append(
            remote.send(
                tokens_hbm.at[:, pl.ds(size - edge_rows, edge_rows), :],
                edge.at[place],
                edge_send.at[d],
                edge_recv.at[d],
                at(after, lax.rem(place + d, peers)),
            )
        )
    maps[...] = jnp.zeros_like(maps)
    started = (me > 0).astype(F32)

    def absorb(h, initial):
        if len(token_mix.shape) == 3:
            mixing = token_mix[h]
        else:
            mixing = token_mix[:, pl.ds(pl.multiple_of(h * own, own), own)]
        currents, changes = [], []
        for s in range(seqs):
            current = wide[h, s].astype(F32)
            row = edge[h, s].astype(F32)[edge_rows - 1 :, :] * started
            earlier = jnp.where(iota(current.shape, 0) == 0, row, pltpu.roll(current, 1, 0))
            currents.append(current)
            changes.append(earlier - current)
        current = jnp.concatenate(currents, axis=0)
        change = jnp.concatenate(changes, axis=0)
        rows = pl.ds(pl.multiple_of(h * own, own), own)
        for j, total, weight in (
            (0, sums[0], weights[0]),
            (2, sums[1], weights[1]),
            (3, sums[2], weights[2]),
            (1, low_sums[0], downs[0]),
            (4, low_sums[1], downs[1]),
        ):
            blended = (current + change * mixing[j : j + 1, :]).astype(BF16)
            term = dot(blended, weight[rows, :])
            total[...] = term if initial else total[...] + term

    own_copy.wait()
    for copy in edges:
        copy.wait_recv()
    for copy in loads[:-1]:
        copy.wait()
    absorb(place, True)
    for copy in from_mate:
        copy.wait_recv()
    absorb(mate, False)
    passed = []
    for s, d, copy in from_across:
        copy.wait_recv()
        came = lax.rem(chip + chips - d, chips) * 2 + core
        passed.append(
            remote.send(
                wide.at[came, s],
                wide.at[came, s],
                pass_send.at[d, s],
                pass_recv.at[d, s],
                at(me, mate),
            )
        )
    for d in range(1, chips):
        absorb(lax.rem(chip + chips - d, chips) * 2 + core, False)
    for copy in passed:
        copy.wait_recv()
    for d in range(1, chips):
        absorb(lax.rem(chip + chips - d, chips) * 2 + 1 - core, False)

    def one(s, carry):
        at_rows = pl.ds(pl.multiple_of(s * size, size), size)
        decay_hidden = jnp.tanh(low_sums[0][at_rows, :]).astype(BF16)
        learn_hidden = low_sums[1][at_rows, :].astype(BF16)
        units = []
        for g in range(width // PAIR):
            lanes = pl.ds(g * PAIR, PAIR)
            units.append(
                chunk_maps(
                    sums[0][at_rows, lanes],
                    sums[1][at_rows, lanes],
                    sums[2][at_rows, lanes],
                    vectors[0][:, lanes] + dot(decay_hidden, ups[0][:, lanes]),
                    vectors[1][:, lanes] + dot(learn_hidden, ups[1][:, lanes]),
                    vectors[2][:, lanes],
                    vectors[3][:, lanes],
                )
            )
        for g, (q, rest, low, high) in enumerate(interleaved(units)):
            lanes = pl.ds(g * PAIR, PAIR)
            query[at_rows, lanes] = q.astype(BF16)
            local[at_rows, lanes] = rest
            pair = s * heads + 2 * g
            maps[pair // n, pair % n] = low.astype(BF16)
            maps[(pair + 1) // n, (pair + 1) % n] = high.astype(BF16)
        return carry

    lax.fori_loop(0, seqs, one, 0)

    def exchange(source, target, send, recv):
        copies = []
        for d in range(1, n):
            there = lax.rem(me + d, n)
            copies.append(
                remote.send(
                    source.at[:, there],
                    target.at[:, me],
                    send.at[d],
                    recv.at[d],
                    at(there, place),
                )
            )
        for slot in range(slots):
            target[slot, me] = source[slot, me]
        for copy in copies:
            copy.wait_recv()

    exchange(maps, got, map_send, map_recv)
    pick = (iota((HEAD_SIZE, PAIR), 0) == iota((HEAD_SIZE, PAIR), 1)).astype(BF16)
    first = iota((HEAD_SIZE, PAIR), 1) < HEAD_SIZE
    packed = [jnp.zeros((HEAD_SIZE, PAIR), BF16)] * slots
    for i in range(n):
        for slot in range(slots):
            states[slot, i] = packed[slot]
        if i == n - 1:
            break
        for slot in range(slots):
            follow = dot(got[slot, i], jnp.concatenate([packed[slot], pick], axis=0))
            whole = follow + pltpu.roll(follow, HEAD_SIZE, 1)
            coarse = whole.astype(BF16)
            fine = (whole - coarse.astype(F32)).astype(BF16)
            packed[slot] = jnp.where(first, coarse, fine)
    exchange(states, entry, state_send, state_recv)

    def finish(s):
        at_rows = pl.ds(s * size, size)
        for g in range(width // PAIR):
            lanes = pl.ds(g * PAIR, PAIR)
            pair = s * heads + 2 * g
            low = entry[pair // n, pair % n]
            high = entry[(pair + 1) // n, (pair + 1) % n]
            zero = jnp.zeros_like(low)
            shifted = jnp.concatenate([zero[:, :HEAD_SIZE], high[:, :HEAD_SIZE]], axis=1)
            both = jnp.concatenate([jnp.where(first, low, zero), shifted], axis=0)
            wkv = local[at_rows, lanes] + dot(query[at_rows, lanes], both)
            normed[at_rows, lanes] = group_norm(
                wkv, vectors[4][:, lanes], vectors[5][:, lanes]
            ).astype(BF16)

    def columns(index):
        if len(output_weight.shape) == 3:
            return output_weight[index]
        return output_weight[:, pl.ds(pl.multiple_of(index * own, own), own)]

    loads[-1].wait()
    order = list(range(1, chips)) + [0]
    to_mate = {}
    for s in range(seqs):
        finish(s)
        at_rows = pl.ds(s * size, size)
        for d in order:
            other = lax.rem(chip + d, chips)
            part[d, s] = dot(normed[at_rows, :], columns(other * 2 + 1 - core)).astype(BF16)
            to_mate[d, s] = remote.send(
                part.at[d, s],
                mate_got.at[d, s],
                mate_send.at[d, s],
                mate_recv.at[d, s],
                at(me, mate),
            )
        for d in order[:-1]:
            other = lax.rem(chip + d, chips)
            mine = dot(normed[at_rows, :], columns(other * 2 + core))
            to_mate[d, s].wait_recv()
            across[d, s] = (mine + mate_got[d, s].astype(F32)).astype(BF16)
            to_mate[d, s, "far"] = remote.send(
                across.at[d, s],
                across_got.at[d, s],
                across_send.at[d, s],
                across_recv.at[d, s],
                at(me, other * 2 + core),
            )
    for s in range(seqs):
        at_rows = pl.ds(s * size, size)
        mine = dot(normed[at_rows, :], columns(place))
        to_mate[0, s].wait_recv()
        mine = mine + mate_got[0, s].astype(F32)
        for d in order[:-1]:
            to_mate[d, s, "far"].wait_recv()
            mine = mine + across_got[d, s].astype(F32)
        out[at_rows, :] = mine.astype(BF16)
    remote.drain()


def layer(tokens, token_mix, weights, downs, ups, vectors, output_weight):
    seqs, size, own = tokens.shape
    rows, width = seqs * size, weights[0].shape[1]
    n, peers = lax.axis_size("seq"), lax.axis_size("head")
    chips = peers // 2
    slots = -(-(seqs * width // HEAD_SIZE) // n)
    edge_rows = min(16, size)
    sems = pltpu.SemaphoreType.DMA
    table = pltpu.VMEM((slots, n, HEAD_SIZE, PAIR), BF16)
    piece = pltpu.VMEM((chips, seqs, size, own), BF16)
    inside = pl.BlockSpec(memory_space=pltpu.VMEM)
    outside = pl.BlockSpec(memory_space=pl.ANY)

    def like(array):
        return pltpu.VMEM(array.shape, array.dtype)

    return pl.pallas_call(
        layer_kernel,
        out_shape=jax.ShapeDtypeStruct((rows, own), BF16),
        in_specs=[outside, inside, [outside] * 3, [outside] * 2, [inside] * 2, [inside] * 6, outside],
        out_specs=inside,
        scratch_shapes=[
            pltpu.VMEM((peers, seqs, size, own), BF16),
            pltpu.VMEM((peers, seqs, edge_rows, own), BF16),
            [like(weight) for weight in weights],
            [like(down) for down in downs],
            like(output_weight),
            [pltpu.VMEM((rows, width), F32)] * 3,
            [pltpu.VMEM((rows, down.shape[1]), F32) for down in downs],
            pltpu.VMEM((rows, width), BF16),
            pltpu.VMEM((rows, width), F32),
            pltpu.VMEM((rows, width), BF16),
            table,
            table,
            table,
            table,
            piece,
            piece,
            piece,
            piece,
            sems((len(weights) + len(downs) + 1,)),
            sems((1,)),
            sems((chips, seqs)),
            sems((chips, seqs)),
            sems((chips, seqs)),
            sems((chips, seqs)),
            sems((peers,)),
            sems((peers,)),
            sems((n,)),
            sems((n,)),
            sems((n,)),
            sems((n,)),
            sems((chips, seqs)),
            sems((chips, seqs)),
            sems((chips, seqs)),
            sems((chips, seqs)),
        ],
        compiler_params=pltpu.CompilerParams(
            collective_id=0, has_side_effects=True, vmem_limit_bytes=56 * 2**20
        ),
    )(tokens, token_mix, weights, downs, ups, vectors, output_weight)


def body(
    tokens,
    token_mix,
    receptance,
    key_weight,
    value_weight,
    decay_base,
    decay_down_matrix,
    decay_up_matrix,
    learn_base,
    learning_down_matrix,
    learning_up_matrix,
    key_scale,
    key_blend,
    norm_gain,
    norm_bias,
    output_weight,
):
    seqs, length, own_width = tokens.shape
    lack = -own_width % PAIR
    if lack:
        wider = lambda array: jnp.pad(array, [(0, 0)] * (array.ndim - 1) + [(0, lack)])
        receptance, key_weight, value_weight, decay_up_matrix, learning_up_matrix = map(
            wider, (receptance, key_weight, value_weight, decay_up_matrix, learning_up_matrix)
        )
        decay_base, learn_base, key_scale, key_blend, norm_gain, norm_bias = map(
            wider, (decay_base, learn_base, key_scale, key_blend, norm_gain, norm_bias)
        )
        output_weight = jnp.pad(output_weight, [(0, lack), (0, 0)])
        output_weight = output_weight.reshape(own_width + lack, -1, own_width).transpose(1, 0, 2)
        token_mix = token_mix.reshape(token_mix.shape[0], -1, own_width).transpose(1, 0, 2)
    vectors = [decay_base, learn_base, key_scale, key_blend, norm_gain, norm_bias]
    result = layer(
        tokens,
        token_mix,
        [receptance, key_weight, value_weight],
        [decay_down_matrix, learning_down_matrix],
        [decay_up_matrix, learning_up_matrix],
        [vector[None] for vector in vectors],
        output_weight,
    )
    return result.reshape(seqs, length, own_width)


def solution(mesh):
    placed = (
        P(None, "seq", "head"),
        P(),
        P(None, "head"),
        P(None, "head"),
        P(None, "head"),
        P("head"),
        P(),
        P(None, "head"),
        P("head"),
        P(),
        P(None, "head"),
        P("head"),
        P("head"),
        P("head"),
        P("head"),
        P("head", None),
    )
    return jax.shard_map(
        body, mesh=mesh, in_specs=placed, out_specs=P(None, "seq", "head"), check_vma=False
    )
```

time: 120 us -> 74.7 us (0.62)
  waiting for transfers between devices: 16.7 us -> 0 us
  between operations: 13.5 us -> 0.01 us
  matrix products: 7.5 us -> 0 us
  other arithmetic: 7.43 us -> 0 us
  local copies, waits for them, and re-layouts: 8.47 us -> 13.6 us
  starting transfers between devices: 4.99 us -> 0 us
    all_gather x1 -> x0, waiting for transfers between devices: 15.4 us -> none  [body(): lax.all_gather(jnp.concatenate([boundary, tokens], axis=1), 'head', axis=...]
    broadcast_in_dim x0 -> x6, local copies, waits for them, and re-layouts: none -> 7.64 us  [body(): vector[None]]
    dot_general x5 -> x0, matrix products: 7.5 us -> none  [dot(): return jnp.dot(left, right, preferred_element_type=F32)]
    convert_element_type x1 -> x0, other arithmetic: 5.63 us -> none  [project(): (current + change * token_mix[which]).astype(BF16).reshape(rows, extent)]
    ppermute x1 -> x0, starting transfers between devices: 4.99 us -> none  [body(): lax.ppermute(tokens[:, length - 1:, :], 'seq', [(i, i + 1) for i in range...]
    another operation x7 -> x0, local copies, waits for them, and re-layouts: 4.17 us -> none  [body(): jnp.stack([decay_base, learn_base, key_scale, key_blend, norm_gain, norm_...]
    unnamed x19 -> x3, local copies, waits for them, and re-layouts: 1.93 us -> 5.96 us
    slice x2 -> x0, local copies, waits for them, and re-layouts: 2.14 us -> none  [the longest x1 1.26 us: project(): token_mix[which]]
  transfers between devices with their start and end apart: 2 -> 0, of which waited for: 2 -> 0; matrix products, arithmetic and copies ran while one was open for 5% -> 0% of each run, Pallas kernels for 0% -> 0%
where the time goes in v1:
time: 74.7 us; the launch traced here: 73.2 us
  Pallas kernels  59.6 us (80%)
  local copies, waits for them, and re-layouts  13.6 us (18%)
    pallas_call x1, Pallas kernels, layer(): pl.pallas_call(layer_kernel, out_shape=jax.ShapeDtypeStruct((rows, own),...  59.6 us
    broadcast_in_dim x6, local copies, waits for them, and re-layouts, body(): vector[None]  7.64 us
    unnamed x3, local copies, waits for them, and re-layouts  5.96 us

profile of v1, /device:TPU:0, one launch (start us, length us, event | category | flops | bytes accessed | tf_op | source)
XLA Modules:
  0.0 73.2 jit_solution(12969667738940886825)
XLA Ops:
  0.0 1.3 %broadcast_in_dim.18.vectors_0_ = f32[1,640]{1,0:T(1,128)} reshape(f32[640]{0:T(1024)} %param.21) | data formatting | bytes 5120 | tf_op jit(solution)/shard_map/broadcast_in_dim | solution.py:569
  1.3 1.3 %broadcast_in_dim.19.vectors_1_ = f32[1,640]{1,0:T(1,128)} reshape(f32[640]{0:T(1024)} %param.24) | data formatting | bytes 5120 | tf_op jit(solution)/shard_map/broadcast_in_dim | solution.py:569
  2.5 1.3 %broadcast_in_dim.20.vectors_2_ = f32[1,640]{1,0:T(1,128)} reshape(f32[640]{0:T(1024)} %param.27) | data formatting | bytes 5120 | tf_op jit(solution)/shard_map/broadcast_in_dim | solution.py:569
  3.8 1.3 %broadcast_in_dim.21.vectors_3_ = f32[1,640]{1,0:T(1,128)} reshape(f32[640]{0:T(1024)} %param.28) | data formatting | bytes 5120 | tf_op jit(solution)/shard_map/broadcast_in_dim | solution.py:569
  5.1 1.3 %broadcast_in_dim.22.vectors_4_ = f32[1,640]{1,0:T(1,128)} reshape(f32[640]{0:T(1024)} %param.29) | data formatting | bytes 5120 | tf_op jit(solution)/shard_map/broadcast_in_dim | solution.py:569
  6.4 1.3 %broadcast_in_dim.23.vectors_5_ = f32[1,640]{1,0:T(1,128)} reshape(f32[640]{0:T(1024)} %param.30) | data formatting | bytes 5120 | tf_op jit(solution)/shard_map/broadcast_in_dim | solution.py:569
  7.6 2.1 %copy.17.downs_hbm_0_ = bf16[2560,96]{1,0:T(8,128)(2,1)} copy(bf16[2560,96]{0,1:T(8,128)(2,1)} %param.22) | data formatting | bytes 983040 | tf_op args[6]
  9.8 2.1 %copy.18.downs_hbm_1_ = bf16[2560,96]{1,0:T(8,128)(2,1)} copy(bf16[2560,96]{0,1:T(8,128)(2,1)} %param.25) | data formatting | bytes 983040 | tf_op args[9]
  11.9 59.6 %shard_map.154 = bf16[256,640]{1,0:T(8,128)(2,1)} custom-call(bf16[2,128,640]{2,1,0:T(8,128)(2,1)} %tokens_hbm.1, f32[5,2560]{1,0:T(8,128)} %token_mix.1, bf16[2560,640]{1,0:T(8,128)(2,1)} %weights_hbm_0_.1, bf16[2560,640]{1,0:T(8,128)(2,1)} %weights_hbm_1_.1, bf16[2560,640]{1,0:T(8,128)(2,1)} %weights_hbm_2_.1, bf16[2560,96]{1,0:T(8,128)(2,1)} %copy.17.downs_hbm_0_, ...), custom_call_target="tpu_custom_call" | custom-call | tf_op jit(solution)/shard_map/pallas_call | solution.py:484
  71.5 1.7 %copy.20 = bf16[2,128,640]{2,1,0:T(8,128)(2,1)} copy(bf16[2,128,640]{2,1,0:T(8,128)(2,1)} %bitcast.1) | data formatting | bytes 655360

commit v2 on v1

--- a/solution.py
+++ b/solution.py
@@ -40,6 +40,12 @@
 
 def diagonal(values):
     half = values.shape[1] // 2
+    if half % PAIR == 0:
+        zero = jnp.zeros_like(values[:, :half])
+        upper = jnp.concatenate([values[:, :half], zero], axis=1)
+        return jnp.concatenate(
+            [upper, jnp.concatenate([zero, values[:, half:]], axis=1)], axis=0
+        )
     first = iota(values.shape, 1) < half
     zero = jnp.zeros_like(values)
     return jnp.concatenate(
@@ -54,7 +60,13 @@
             return results
 
 
-def chunk_maps(recept, key_raw, value, decay_arg, learn_arg, key_scale, key_blend):
+def link_masks(size):
+    crossing = iota((size, 2 * size), 0) ^ (iota((size, 2 * size), 1) % size)
+    blocks = [2**level for level in range((size - 1).bit_length())]
+    return [((crossing >= b) & (crossing < 2 * b)).astype(F32).astype(BF16) for b in blocks]
+
+
+def chunk_maps(masks, recept, key_raw, value, decay_arg, learn_arg, key_scale, key_blend):
     size = recept.shape[0]
     decay = -DECAY_SCALE / (1.0 + jnp.exp(-decay_arg))
     learn = 1.0 / (1.0 + jnp.exp(-learn_arg))
@@ -86,20 +98,14 @@
     lower_ak = jnp.where(strict, with_key[:size], 0.0).astype(BF16)
     lower_rb = jnp.where(within, with_beta[size:], 0.0).astype(BF16)
     lower_rk = jnp.where(within, with_key[size:], 0.0).astype(BF16)
-    zero = jnp.zeros_like(lower_ab)
-    crossing = row ^ column
-    inverse = jnp.where(row == column, 1.0, 0.0) + jnp.where(
-        crossing == 1, lower_ab, zero
-    ).astype(F32)
-    block = 2
-    while block < size:
-        link = jnp.where((crossing >= block) & (crossing < 2 * block), lower_ab, zero)
+    inverse = jnp.where(row == column, 1.0, 0.0) + (lower_ab * masks[0]).astype(F32)
+    for mask in masks[1:]:
+        link = lower_ab * mask
         rounded = inverse.astype(BF16)
         half = dot(rounded, diagonal(link)).astype(BF16)
         yield
         inverse = inverse + dot(half, diagonal(rounded))
         yield
-        block *= 2
     yield
     value_b = value.astype(BF16)
     from_value = dot(jnp.concatenate([lower_ak, lower_rk], axis=0), diagonal(value_b))
@@ -222,6 +228,9 @@
     edge_rows = edge.shape[2]
     remote = Remote()
 
+    def row_of(which, lanes):
+        return vectors[which][lanes].reshape(1, PAIR)
+
     def at(seq, head):
         return {"seq": seq, "head": head}
 
@@ -250,6 +259,20 @@
         greet(before, lax.rem(place + d, peers))
     pl.semaphore_wait(barrier, n - 1 + chips + peers - 1)
 
+    edges = {}
+
+    def send_edge(d, swap):
+        to_core = 1 - core if swap else core
+        edges[d, swap] = remote.send(
+            tokens_hbm.at[:, pl.ds(size - edge_rows, edge_rows), :],
+            edge.at[place],
+            edge_send.at[2 * d + swap],
+            edge_recv.at[2 * d + swap],
+            at(after, lax.rem(chip + d, chips) * 2 + to_core),
+        )
+
+    send_edge(0, 0)
+    send_edge(0, 1)
     from_across = []
     for s in range(seqs):
         for d in range(1, chips):
@@ -272,17 +295,9 @@
                 at(me, mate),
             )
         )
-    edges = []
-    for d in range(peers):
-        edges.append(
-            remote.send(
-                tokens_hbm.at[:, pl.ds(size - edge_rows, edge_rows), :],
-                edge.at[place],
-                edge_send.at[d],
-                edge_recv.at[d],
-                at(after, lax.rem(place + d, peers)),
-            )
-        )
+    for d in range(1, chips):
+        send_edge(d, 0)
+        send_edge(d, 1)
     maps[...] = jnp.zeros_like(maps)
     started = (me > 0).astype(F32)
 
@@ -309,17 +324,22 @@
             (4, low_sums[1], downs[1]),
         ):
             blended = (current + change * mixing[j : j + 1, :]).astype(BF16)
-            term = dot(blended, weight[rows, :])
+            if j in (0, 2, 3):
+                term = dot(blended, weight[rows, :])
+            elif len(weight.shape) == 3:
+                term = dot_nt(blended, weight[h])
+            else:
+                term = dot_nt(blended, weight[:, pl.ds(pl.multiple_of(h * own, own), own)])
             total[...] = term if initial else total[...] + term
 
     own_copy.wait()
-    for copy in edges:
-        copy.wait_recv()
     for copy in loads[:-1]:
         copy.wait()
+    edges[0, 0].wait_recv()
     absorb(place, True)
     for copy in from_mate:
         copy.wait_recv()
+    edges[0, 1].wait_recv()
     absorb(mate, False)
     passed = []
     for s, d, copy in from_across:
@@ -335,14 +355,18 @@
             )
         )
     for d in range(1, chips):
+        edges[d, 0].wait_recv()
         absorb(lax.rem(chip + chips - d, chips) * 2 + core, False)
     for copy in passed:
         copy.wait_recv()
     for d in range(1, chips):
+        edges[d, 1].wait_recv()
         absorb(lax.rem(chip + chips - d, chips) * 2 + 1 - core, False)
 
-    def one(s, carry):
-        at_rows = pl.ds(pl.multiple_of(s * size, size), size)
+    masks = link_masks(size)
+
+    def one(s):
+        at_rows = pl.ds(s * size, size)
         decay_hidden = jnp.tanh(low_sums[0][at_rows, :]).astype(BF16)
         learn_hidden = low_sums[1][at_rows, :].astype(BF16)
         units = []
@@ -350,13 +374,14 @@
             lanes = pl.ds(g * PAIR, PAIR)
             units.append(
                 chunk_maps(
+                    masks,
                     sums[0][at_rows, lanes],
                     sums[1][at_rows, lanes],
                     sums[2][at_rows, lanes],
-                    vectors[0][:, lanes] + dot(decay_hidden, ups[0][:, lanes]),
-                    vectors[1][:, lanes] + dot(learn_hidden, ups[1][:, lanes]),
-                    vectors[2][:, lanes],
-                    vectors[3][:, lanes],
+                    row_of(0, lanes) + dot(decay_hidden, ups[0][:, lanes]),
+                    row_of(1, lanes) + dot(learn_hidden, ups[1][:, lanes]),
+                    row_of(2, lanes),
+                    row_of(3, lanes),
                 )
             )
         for g, (q, rest, low, high) in enumerate(interleaved(units)):
@@ -366,44 +391,62 @@
             pair = s * heads + 2 * g
             maps[pair // n, pair % n] = low.astype(BF16)
             maps[(pair + 1) // n, (pair + 1) % n] = high.astype(BF16)
-        return carry
-
-    lax.fori_loop(0, seqs, one, 0)
-
-    def exchange(source, target, send, recv):
+
+    early = heads // n
+    groups = [(0, early), (early, slots)] if early else [(0, slots)]
+
+    def exchange(group, source, target, send, recv):
+        low, high = groups[group]
+        some = pl.ds(low, high - low)
         copies = []
         for d in range(1, n):
             there = lax.rem(me + d, n)
             copies.append(
                 remote.send(
-                    source.at[:, there],
-                    target.at[:, me],
-                    send.at[d],
-                    recv.at[d],
+                    source.at[some, there],
+                    target.at[some, me],
+                    send.at[group, d],
+                    recv.at[group, d],
                     at(there, place),
                 )
             )
-        for slot in range(slots):
+        for slot in range(low, high):
             target[slot, me] = source[slot, me]
-        for copy in copies:
-            copy.wait_recv()
-
-    exchange(maps, got, map_send, map_recv)
+        return copies
+
     pick = (iota((HEAD_SIZE, PAIR), 0) == iota((HEAD_SIZE, PAIR), 1)).astype(BF16)
     first = iota((HEAD_SIZE, PAIR), 1) < HEAD_SIZE
-    packed = [jnp.zeros((HEAD_SIZE, PAIR), BF16)] * slots
-    for i in range(n):
-        for slot in range(slots):
-            states[slot, i] = packed[slot]
-        if i == n - 1:
-            break
-        for slot in range(slots):
-            follow = dot(got[slot, i], jnp.concatenate([packed[slot], pick], axis=0))
-            whole = follow + pltpu.roll(follow, HEAD_SIZE, 1)
-            coarse = whole.astype(BF16)
-            fine = (whole - coarse.astype(F32)).astype(BF16)
-            packed[slot] = jnp.where(first, coarse, fine)
-    exchange(states, entry, state_send, state_recv)
+
+    def scan(group):
+        members = range(*groups[group])
+        packed = {slot: jnp.zeros((HEAD_SIZE, PAIR), BF16) for slot in members}
+        for i in range(n):
+            for slot in members:
+                states[slot, i] = packed[slot]
+            if i == n - 1:
+                break
+            for slot in members:
+                follow = dot(got[slot, i], jnp.concatenate([packed[slot], pick], axis=0))
+                whole = follow + pltpu.roll(follow, HEAD_SIZE, 1)
+                coarse = whole.astype(BF16)
+                fine = (whole - coarse.astype(F32)).astype(BF16)
+                packed[slot] = jnp.where(first, coarse, fine)
+
+    arriving = {}
+    for s in range(seqs):
+        one(s)
+        if s == 0 and early:
+            arriving[0] = exchange(0, maps, got, map_send, map_recv)
+    last = len(groups) - 1
+    arriving[last] = exchange(last, maps, got, map_send, map_recv)
+    returning = []
+    for group in range(len(groups)):
+        for copy in arriving[group]:
+            copy.wait_recv()
+        scan(group)
+        returning += exchange(group, states, entry, state_send, state_recv)
+    for copy in returning:
+        copy.wait_recv()
 
     def finish(s):
         at_rows = pl.ds(s * size, size)
@@ -417,7 +460,7 @@
             both = jnp.concatenate([jnp.where(first, low, zero), shifted], axis=0)
             wkv = local[at_rows, lanes] + dot(query[at_rows, lanes], both)
             normed[at_rows, lanes] = group_norm(
-                wkv, vectors[4][:, lanes], vectors[5][:, lanes]
+                wkv, row_of(4, lanes), row_of(5, lanes)
             ).astype(BF16)
 
     def columns(index):
@@ -493,7 +536,7 @@
             [like(down) for down in downs],
             like(output_weight),
             [pltpu.VMEM((rows, width), F32)] * 3,
-            [pltpu.VMEM((rows, down.shape[1]), F32) for down in downs],
+            [pltpu.VMEM((rows, down.shape[-2]), F32) for down in downs],
             pltpu.VMEM((rows, width), BF16),
             pltpu.VMEM((rows, width), F32),
             pltpu.VMEM((rows, width), BF16),
@@ -513,10 +556,10 @@
             sems((chips, seqs)),
             sems((peers,)),
             sems((peers,)),
-            sems((n,)),
-            sems((n,)),
-            sems((n,)),
-            sems((n,)),
+            sems((2, n)),
+            sems((2, n)),
+            sems((2, n)),
+            sems((2, n)),
             sems((chips, seqs)),
             sems((chips, seqs)),
             sems((chips, seqs)),
@@ -559,14 +602,17 @@
         output_weight = jnp.pad(output_weight, [(0, lack), (0, 0)])
         output_weight = output_weight.reshape(own_width + lack, -1, own_width).transpose(1, 0, 2)
         token_mix = token_mix.reshape(token_mix.shape[0], -1, own_width).transpose(1, 0, 2)
+    downs = [decay_down_matrix.T, learning_down_matrix.T]
+    if lack:
+        downs = [down.reshape(down.shape[0], -1, own_width).transpose(1, 0, 2) for down in downs]
     vectors = [decay_base, learn_base, key_scale, key_blend, norm_gain, norm_bias]
     result = layer(
         tokens,
         token_mix,
         [receptance, key_weight, value_weight],
-        [decay_down_matrix, learning_down_matrix],
+        downs,
         [decay_up_matrix, learning_up_matrix],
-        [vector[None] for vector in vectors],
+        vectors,
         output_weight,
     )
     return result.reshape(seqs, length, own_width)

time: 74.7 us -> 56.3 us (0.75); the launches traced: 73.2 us -> 56.1 us
  local copies, waits for them, and re-layouts: 13.6 us -> 1.73 us
  Pallas kernels: 59.6 us -> 54.4 us
    broadcast_in_dim x6 -> x0, local copies, waits for them, and re-layouts: 7.64 us -> none  [body(): vector[None]]
    pallas_call x1, Pallas kernels: 59.6 us -> 54.4 us  [layer(): pl.pallas_call(layer_kernel, out_shape=jax.ShapeDtypeStruct((rows, own),...]
    unnamed x3 -> x1, local copies, waits for them, and re-layouts: 5.96 us -> 1.73 us
where the time goes in v2:
time: 56.3 us; the launch traced here: 56.1 us
  Pallas kernels  54.4 us (97%)
  local copies, waits for them, and re-layouts  1.73 us (3%)
    pallas_call x1, Pallas kernels, layer(): pl.pallas_call(layer_kernel, out_shape=jax.ShapeDtypeStruct((rows, own),...  54.4 us
    unnamed x1, local copies, waits for them, and re-layouts  1.73 us

profile of v2, /device:TPU:0, one launch (start us, length us, event | category | flops | bytes accessed | tf_op | source)
XLA Modules:
  0.0 56.1 jit_solution(10125805455863572351)
XLA Ops:
  0.0 54.4 %shard_map.154 = bf16[256,640]{1,0:T(8,128)(2,1)} custom-call(bf16[2,128,640]{2,1,0:T(8,128)(2,1)} %tokens_hbm.1, f32[5,2560]{1,0:T(8,128)} %token_mix.1, bf16[2560,640]{1,0:T(8,128)(2,1)} %weights_hbm_0_.1, bf16[2560,640]{1,0:T(8,128)(2,1)} %weights_hbm_1_.1, bf16[2560,640]{1,0:T(8,128)(2,1)} %weights_hbm_2_.1, bf16[96,2560]{1,0:T(8,128)(2,1)} %bitcast.4, ...), custom_call_target="tpu_custom_call" | custom-call | tf_op jit(solution)/shard_map/pallas_call | solution.py:527
  54.4 1.7 %copy.18 = bf16[2,128,640]{2,1,0:T(8,128)(2,1)} copy(bf16[2,128,640]{2,1,0:T(8,128)(2,1)} %bitcast.3) | data formatting | bytes 655360

commit v3 on v2

--- a/solution.py
+++ b/solution.py
@@ -316,14 +316,16 @@
         current = jnp.concatenate(currents, axis=0)
         change = jnp.concatenate(changes, axis=0)
         rows = pl.ds(pl.multiple_of(h * own, own), own)
-        for j, total, weight in (
-            (0, sums[0], weights[0]),
-            (2, sums[1], weights[1]),
-            (3, sums[2], weights[2]),
-            (1, low_sums[0], downs[0]),
-            (4, low_sums[1], downs[1]),
+        for load, j, total, weight in (
+            (loads[0], 0, sums[0], weights[0]),
+            (loads[1], 2, sums[1], weights[1]),
+            (loads[2], 3, sums[2], weights[2]),
+            (loads[3], 1, low_sums[0], downs[0]),
+            (loads[4], 4, low_sums[1], downs[1]),
         ):
             blended = (current + change * mixing[j : j + 1, :]).astype(BF16)
+            if initial:
+                load.wait()
             if j in (0, 2, 3):
                 term = dot(blended, weight[rows, :])
             elif len(weight.shape) == 3:
@@ -333,8 +335,6 @@
             total[...] = term if initial else total[...] + term
 
     own_copy.wait()
-    for copy in loads[:-1]:
-        copy.wait()
     edges[0, 0].wait_recv()
     absorb(place, True)
     for copy in from_mate:

time: 56.3 us -> 56.5 us (level)
  no operation moved by 1% of the time
where the time goes in v3:
time: 56.5 us; the launch traced here: 56.3 us
  Pallas kernels  54.6 us (97%)
  local copies, waits for them, and re-layouts  1.73 us (3%)
    pallas_call x1, Pallas kernels, layer(): pl.pallas_call(layer_kernel, out_shape=jax.ShapeDtypeStruct((rows, own),...  54.6 us
    unnamed x1, local copies, waits for them, and re-layouts  1.73 us

profile of v3, /device:TPU:0, one launch (start us, length us, event | category | flops | bytes accessed | tf_op | source)
XLA Modules:
  0.0 56.3 jit_solution(11033891366175571610)
XLA Ops:
  0.0 54.6 %shard_map.154 = bf16[256,640]{1,0:T(8,128)(2,1)} custom-call(bf16[2,128,640]{2,1,0:T(8,128)(2,1)} %tokens_hbm.1, f32[5,2560]{1,0:T(8,128)} %token_mix.1, bf16[2560,640]{1,0:T(8,128)(2,1)} %weights_hbm_0_.1, bf16[2560,640]{1,0:T(8,128)(2,1)} %weights_hbm_1_.1, bf16[2560,640]{1,0:T(8,128)(2,1)} %weights_hbm_2_.1, bf16[96,2560]{1,0:T(8,128)(2,1)} %bitcast.4, ...), custom_call_target="tpu_custom_call" | custom-call | tf_op jit(solution)/shard_map/pallas_call | solution.py:527
  54.6 1.7 %copy.18 = bf16[2,128,640]{2,1,0:T(8,128)(2,1)} copy(bf16[2,128,640]{2,1,0:T(8,128)(2,1)} %bitcast.3) | data formatting | bytes 655360
